TPU v7x, 512 devices: a whole 4x8x8 slice. The times are simulated.
512 devices in a mesh: slab: 64 (over x, y, core), cross: 8 (over z).
Axes of the slice: x: 4, y: 8, z: 8, core: 2. Of those that a mesh axis runs over, the one named last changes fastest.
Arguments:
- positions: int32 [3, 8388608], P(None, ('slab', 'cross')), may hold values from 0 to 2047, as said below
- velocities: float32 [3, 8388608], P(None, ('slab', 'cross')), may hold values from -6 to 6
- counts: int32 [512], P(('slab', 'cross')), may hold values from 1025 to 16384, as said below
- grid_shift: int32 [3], replicated, may hold values from -4 to 3
- axis_index: int32 [256, 256, 128], P('slab', 'cross'), may hold values from 0 to 5
- droplet: int32 [256, 256, 128], P('slab', 'cross'), may hold values 0 or 1
Outputs:
- new_velocities: float32 [3, 8388608], P(None, ('slab', 'cross'))
Inputs may be any that keep to these rules, and one draw needn't show every extreme that they name: `counts`: live particles of a device are in its first slots; one device has 16384 live particles and one has 1025. `positions`: the particles in the slots of device (i, j) of the slab and cross axes lie within half a cell of its block: x within [i * 4 * 8 - 8 // 2, (i + 1) * 4 * 8 + 8 // 2) and y likewise with j and 32, taken periodically; components lie in [0, 2048), [0, 2048), [0, 1024).
All inputs are finite; a program needn't handle non-finite values. No bound on the sum of `droplet` on one device may be relied on, other than what follows from the above.
Results may differ from a plain program's by a relative error of at most 0.00002.
Values sent between devices are 32-bit elements; how exact they have to be, the bound alone decides.
A program may use at most 64 MiB of HBM per device.

v0:
```python
import math

import jax
import jax.numpy as jnp
from jax import lax
from jax.sharding import PartitionSpec as P

QUANT = 8
NFILL = 8


ANGLE = 130.0 * math.pi / 180.0


def with_halo(block, sides, width):
    for axis, dim in sides:
        count = lax.axis_size(axis)
        forward = [(i, i + 1) for i in range(count - 1)]
        forward.append((count - 1, 0))
        backward = [(target, source) for source, target in forward]
        low = lax.ppermute(
            lax.slice_in_dim(block, block.shape[dim] - width, None, axis=dim), axis, forward
        )
        high = lax.ppermute(lax.slice_in_dim(block, 0, width, axis=dim), axis, backward)
        block = jnp.concatenate([low, block, high], axis=dim)
    return block


def shifted(value, axis, steps):
    count = lax.axis_size(axis)
    pairs = [(source, (source + steps) % count) for source in range(count)]
    return lax.ppermute(value, axis, pairs)


def collide(velocity, cell_mean, axis_code):
    relative = velocity - cell_mean
    axis_along = axis_code // 2
    handed = 1.0 - 2.0 * (axis_code % 2).astype(jnp.float32)
    zeros_row = jnp.zeros_like(relative[0])
    cross_first = jnp.where(
        axis_along == 1,
        handed * relative[2],
        jnp.where(axis_along == 2, -handed * relative[1], zeros_row),
    )
    cross_second = jnp.where(
        axis_along == 0,
        -handed * relative[2],
        jnp.where(axis_along == 2, handed * relative[0], zeros_row),
    )
    cross_third = jnp.where(
        axis_along == 0,
        handed * relative[1],
        jnp.where(axis_along == 1, -handed * relative[0], zeros_row),
    )
    crossed = jnp.stack([cross_first, cross_second, cross_third])
    parallel = jnp.stack([axis_along == 0, axis_along == 1, axis_along == 2])
    rotated = jnp.where(parallel, relative, math.cos(ANGLE) * relative + math.sin(ANGLE) * crossed)
    return cell_mean + rotated


def local_cells(positions, grid_shift, planes_x, planes_y, depth_cells):
    slab_anchor = lax.axis_index("slab") * (planes_x * QUANT)
    column_anchor = lax.axis_index("cross") * (planes_y * QUANT)
    period_x = planes_x * lax.axis_size("slab") * QUANT
    period_y = planes_y * lax.axis_size("cross") * QUANT
    offset_x = (positions[0] - slab_anchor + QUANT) % period_x - QUANT
    offset_y = (positions[1] - column_anchor + QUANT) % period_y - QUANT
    index_x = (offset_x + grid_shift[0] + QUANT) // QUANT
    index_y = (offset_y + grid_shift[1] + QUANT) // QUANT
    index_z = (positions[2] + grid_shift[2]) // QUANT % depth_cells
    return (index_x * (planes_y + 2) + index_y) * depth_cells + index_z


def deposit(cell_ids, velocity_part, weight, cell_count):
    parts_list = [jax.ops.segment_sum(weight, cell_ids, num_segments=cell_count)]
    parts_list = parts_list + [
        jax.ops.segment_sum(velocity_part[k] * weight, cell_ids, num_segments=cell_count)
        for k in range(3)
    ]
    return jnp.stack(parts_list)


def body(positions, velocities, counts, grid_shift, axis_index, droplet):
    planes_x, planes_y, depth_cells = axis_index.shape
    capacity = positions.shape[1]
    cell_count = (planes_x + 2) * (planes_y + 2) * depth_cells
    cell_ids = local_cells(positions, grid_shift, planes_x, planes_y, depth_cells)
    living = jnp.arange(capacity, dtype=jnp.int32) < counts[0]
    flag_stack = with_halo(jnp.stack([axis_index, droplet]), (("slab", 1), ("cross", 2)), 1)
    weight = jnp.where(living, 1.0, 0.0).astype(jnp.float32)
    momentum = deposit(cell_ids, velocities, weight, cell_count)
    partial_grid = momentum.reshape(4, planes_x + 2, planes_y + 2, depth_cells)
    from_below = shifted(partial_grid[:, planes_x + 1 : planes_x + 2], "slab", 1)
    from_above = shifted(partial_grid[:, 0:1], "slab", -1)
    partial_grid = (
        partial_grid.at[:, 1:2].add(from_below).at[:, planes_x : planes_x + 1].add(from_above)
    )
    owned_planes = partial_grid[:, 1 : planes_x + 1]
    from_below = shifted(owned_planes[:, :, planes_y + 1 : planes_y + 2], "cross", 1)
    from_above = shifted(owned_planes[:, :, 0:1], "cross", -1)
    owned_sums = (
        owned_planes[:, :, 1 : planes_y + 1]
        .at[:, :, 0:1]
        .add(from_below)
        .at[:, :, planes_y - 1 : planes_y]
        .add(from_above)
    )
    fill_level = jnp.where(droplet == 1, float(NFILL), 1.0).astype(jnp.float32)
    owned_mean = owned_sums[1:4] / jnp.maximum(owned_sums[0], fill_level)
    cell_mean = with_halo(owned_mean, (("slab", 1), ("cross", 2)), 1)
    mean_flat = cell_mean.reshape(3, cell_count)
    code_flat = flag_stack[0].reshape(cell_count)
    collided = collide(
        velocities, jnp.take(mean_flat, cell_ids, axis=1), jnp.take(code_flat, cell_ids)
    )
    return jnp.where(living, collided, 0.0)


def solution(mesh):
    placed = (
        P(None, ("slab", "cross")),
        P(None, ("slab", "cross")),
        P(("slab", "cross")),
        P(),
        P("slab", "cross", None),
        P("slab", "cross", None),
    )
    return jax.shard_map(
        body, mesh=mesh, in_specs=placed, out_specs=P(None, ("slab", "cross")), check_vma=False
    )
```

profile of v0, /device:TPU:448, one launch (start us, length us, event | category | flops | bytes accessed | tf_op | source)
XLA Modules:
  0.0 570.6 jit_solution(9431003218082838642)
XLA Ops:
  0.0 1.4 fusion.63
  1.4 1.5 fusion.61
  3.6 4.9 compare_select_fusion.1
  8.5 85.8 %scatter_custom_fusion = f32[26112]{0:T(1024)S(1)} fusion(s32[16384]{0:T(1024)S(1)} %bitcast.64, f32[16384]{0:T(1024)S(1)} %get-tuple-element.87, f32[]{:T(128)} %constant.256.clone.1), kind=kCustom, calls=%fused_computation.161 | custom fusion | flops 16384 | bytes 104452 | tf_op jit(solution)/shard_map/scatter-add | solution.py:75
  94.3 85.8 %scatter_custom_fusion.1 = f32[26112]{0:T(1024)S(1)} fusion(s32[16384]{0:T(1024)S(1)} %bitcast.65, f32[16384]{0:T(1024)S(1)} %get-tuple-element.86, f32[]{:T(128)} %constant.256.clone.1), kind=kCustom, calls=%fused_computation.159 | custom fusion | flops 16384 | bytes 104452 | tf_op jit(solution)/shard_map/scatter-add | solution.py:77
  180.1 85.8 %scatter_custom_fusion.2 = f32[26112]{0:T(1024)S(1)} fusion(s32[16384]{0:T(1024)S(1)} %bitcast.66, f32[16384]{0:T(1024)S(1)} %get-tuple-element.85, f32[]{:T(128)} %constant.256.clone.1), kind=kCustom, calls=%fused_computation.157 | custom fusion | flops 16384 | bytes 104452 | tf_op jit(solution)/shard_map/scatter-add | solution.py:77
  266.0 85.8 %scatter_custom_fusion.3 = f32[26112]{0:T(1024)S(1)} fusion(s32[16384]{0:T(1024)S(1)} %bitcast.67, f32[16384]{0:T(1024)S(1)} %get-tuple-element.84, f32[]{:T(128)} %constant.256.clone.1), kind=kCustom, calls=%fused_computation.155 | custom fusion | flops 16384 | bytes 104452 | tf_op jit(solution)/shard_map/scatter-add | solution.py:77
  351.8 1.9 collective-permute-start
  353.8 0.8 pad_add_fusion.6
  354.6 3.6 collective-permute-start.8
  358.1 5.3 collective-permute-start.9
  363.5 1.5 iota_compare_fusion
  365.0 2.6 collective-permute-start.1
  367.6 0.8 pad_add_fusion.10
  368.4 1.9 collective-permute-start.10
  370.4 3.9 collective-permute-start.11
  374.3 3.1 collective-permute-start.2
  377.5 0.9 pad_add_fusion
  378.4 90.5 %gather_fusion.1 = s32[16384]{0:T(1024)S(1)} fusion(s32[26112]{0:T(1024)S(1)} %reshape_squeeze.3, s32[16384]{0:T(1024)S(1)} %broadcast_clamp_fusion), kind=kCustom, calls=%fused_computation.1 | custom fusion | bytes 196608 | tf_op jit(solution)/shard_map/jit(_take)/gather | solution.py:114
  469.0 2.7 collective-permute-start.3
  471.8 3.9 collective-permute-done.3
  475.9 1.9 collective-permute-start.4
  477.8 7.0 %collective-permute-start.5 = (f32[3,1,32,128]{3,2,1,0:T(8,128)S(1)}, f32[3,1,32,128]{3,2,1,0:T(8,128)S(1)}, u32[]{:S(2)}, u32[]{:S(2)}) collective-permute-start(f32[3,1,32,128]{3,2,1,0:T(8,128)S(1)} %get-tuple-element.76), channel_id=1, source_target_pairs={{8,0},{16,8},{24,16},{32,24},{40,32},{48,40},{56,48},{64,56},{72,6... | collective-permute-start | bytes 147464 | tf_op jit(solution)/shard_map/ppermute | solution.py:24
  484.8 3.3 broadcast_compare_fusion.2
  488.1 1.9 collective-permute-start.6
  490.1 4.1 collective-permute-start.7
  494.3 2.5 collective-permute-done.7
  496.9 7.0 %copy.67 = f32[3,6,34,128]{0,3,2,1:T(8,128)} copy(f32[3,6,34,128]{3,2,1,0:T(8,128)S(1)} %pad_maximum_fusion) | data formatting | bytes 626688 | tf_op jit(solution)/shard_map/concatenate | solution.py:25
  503.9 59.3 %gather_fusion = f32[16384,3]{1,0:T(8,128)} fusion(f32[3,26112]{0,1:T(8,128)} %bitcast.49, s32[16384]{0:T(1024)S(1)} %broadcast_clamp_fusion), kind=kCustom, calls=%fused_computation | custom fusion | bytes 458752 | tf_op jit(solution)/shard_map/jit(_take)/gather | solution.py:114
  563.2 5.4 copy.68
  568.8 0.5 select_select_fusion.2
  569.3 1.3 fusion.3
  (42 shorter events, 0.8 us)
Async XLA Ops:
  351.8 13.1 %collective-permute-start = (f32[4,1,34,128]{3,2,1,0:T(8,128)S(1)}, f32[4,1,34,128]{3,2,1,0:T(8,128)S(1)}, u32[]{:S(2)}, u32[]{:S(2)}) collective-permute-start(f32[4,1,34,128]{3,2,1,0:T(8,128)S(1)} %slice.245), channel_id=1, source_target_pairs={{0,8},{8,16},{16,24},{24,32},{32,40},{40,48},{48,56},{56,64},{64,7... | collective-permute-start | bytes 208904 | tf_op jit(solution)/shard_map/ppermute | solution.py:32
  354.6 13.1 %collective-permute-start.8 = (s32[2,1,32,128]{3,2,1,0:T(8,128)S(1)}, s32[2,1,32,128]{3,2,1,0:T(8,128)S(1)}, u32[]{:S(2)}, u32[]{:S(2)}) collective-permute-start(s32[2,1,32,128]{3,2,1,0:T(8,128)S(1)} %get-tuple-element.77), channel_id=1, source_target_pairs={{0,8},{8,16},{16,24},{24,32},{32,40},{40,48},{48,56},{56,64},{64,7... | collective-permute-start | bytes 98312 | tf_op jit(solution)/shard_map/ppermute | solution.py:21
  358.1 9.5 %collective-permute-start.9 = (s32[2,1,32,128]{3,2,1,0:T(8,128)S(1)}, s32[2,1,32,128]{3,2,1,0:T(8,128)S(1)}, u32[]{:S(2)}, u32[]{:S(2)}) collective-permute-start(s32[2,1,32,128]{3,2,1,0:T(8,128)S(1)} %get-tuple-element.78), channel_id=1, source_target_pairs={{8,0},{16,8},{24,16},{32,24},{40,32},{48,40},{56,48},{64,56},{72,6... | collective-permute-start | bytes 98312 | tf_op jit(solution)/shard_map/ppermute | solution.py:24
  365.0 9.3 %collective-permute-start.1 = (f32[4,1,34,128]{3,2,1,0:T(8,128)S(1)}, f32[4,1,34,128]{3,2,1,0:T(8,128)S(1)}, u32[]{:S(2)}, u32[]{:S(2)}) collective-permute-start(f32[4,1,34,128]{3,2,1,0:T(8,128)S(1)} %get-tuple-element.63), channel_id=1, source_target_pairs={{0,504},{8,0},{16,8},{24,16},{32,24},{40,32},{48,40},{56,48},{64,5... | collective-permute-start | bytes 208904 | tf_op jit(solution)/shard_map/ppermute | solution.py:32
  368.4 9.1 %collective-permute-start.10 = (s32[2,6,1,128]{3,2,1,0:T(1,128)S(1)}, s32[2,6,1,128]{3,2,1,0:T(1,128)S(1)}, u32[]{:S(2)}, u32[]{:S(2)}) collective-permute-start(s32[2,6,1,128]{3,2,1,0:T(1,128)S(1)} %get-tuple-element.73), channel_id=1, source_target_pairs={{0,1},{1,2},{2,3},{3,4},{4,5},{5,6},{6,7},{7,0},{8,9},{9,10},{10,1... | collective-permute-start | bytes 18440 | tf_op jit(solution)/shard_map/ppermute | solution.py:21
  370.4 7.1 %collective-permute-start.11 = (s32[2,6,1,128]{3,2,1,0:T(1,128)S(1)}, s32[2,6,1,128]{3,2,1,0:T(1,128)S(1)}, u32[]{:S(2)}, u32[]{:S(2)}) collective-permute-start(s32[2,6,1,128]{3,2,1,0:T(1,128)S(1)} %get-tuple-element.74), channel_id=1, source_target_pairs={{1,0},{2,1},{3,2},{4,3},{5,4},{6,5},{7,6},{0,7},{9,8},{10,9},{11,1... | collective-permute-start | bytes 18440 | tf_op jit(solution)/shard_map/ppermute | solution.py:24
  374.3 97.4 %collective-permute-start.2 = (f32[4,4,1,128]{3,2,1,0:T(1,128)S(1)}, f32[4,4,1,128]{3,2,1,0:T(1,128)S(1)}, u32[]{:S(2)}, u32[]{:S(2)}) collective-permute-start(f32[4,4,1,128]{3,2,1,0:T(1,128)S(1)} %get-tuple-element.62), channel_id=1, source_target_pairs={{0,1},{1,2},{2,3},{3,4},{4,5},{5,6},{6,7},{7,0},{8,9},{9,10},{10,1... | collective-permute-start | bytes 24584 | tf_op jit(solution)/shard_map/ppermute | solution.py:32
  378.4 97.4 %copy-start.1 = (s32[4,32,128]{2,1,0:T(8,128)S(1)}, s32[4,32,128]{2,1,0:T(8,128)}, u32[]{:S(2)}) copy-start(s32[4,32,128]{2,1,0:T(8,128)} %param.19) | copy-start | bytes 196612
  469.0 6.8 %collective-permute-start.3 = (f32[4,4,1,128]{3,2,1,0:T(1,128)S(1)}, f32[4,4,1,128]{3,2,1,0:T(1,128)S(1)}, u32[]{:S(2)}, u32[]{:S(2)}) collective-permute-start(f32[4,4,1,128]{3,2,1,0:T(1,128)S(1)} %get-tuple-element.61), channel_id=1, source_target_pairs={{0,7},{1,0},{2,1},{3,2},{4,3},{5,4},{6,5},{7,6},{8,15},{9,8},{10,9... | collective-permute-start | bytes 24584 | tf_op jit(solution)/shard_map/ppermute | solution.py:32
  475.9 12.2 %collective-permute-start.4 = (f32[3,1,32,128]{3,2,1,0:T(8,128)S(1)}, f32[3,1,32,128]{3,2,1,0:T(8,128)S(1)}, u32[]{:S(2)}, u32[]{:S(2)}) collective-permute-start(f32[3,1,32,128]{3,2,1,0:T(8,128)S(1)} %get-tuple-element.75), channel_id=1, source_target_pairs={{0,8},{8,16},{16,24},{24,32},{32,40},{40,48},{48,56},{56,64},{64,7... | collective-permute-start | bytes 147464 | tf_op jit(solution)/shard_map/ppermute | solution.py:21
  477.8 10.3 %collective-permute-start.5 = (f32[3,1,32,128]{3,2,1,0:T(8,128)S(1)}, f32[3,1,32,128]{3,2,1,0:T(8,128)S(1)}, u32[]{:S(2)}, u32[]{:S(2)}) collective-permute-start(f32[3,1,32,128]{3,2,1,0:T(8,128)S(1)} %get-tuple-element.76), channel_id=1, source_target_pairs={{8,0},{16,8},{24,16},{32,24},{40,32},{48,40},{56,48},{64,56},{72,6... | collective-permute-start | bytes 147464 | tf_op jit(solution)/shard_map/ppermute | solution.py:24
  488.1 6.2 %collective-permute-start.6 = (f32[3,6,1,128]{3,2,1,0:T(1,128)S(1)}, f32[3,6,1,128]{3,2,1,0:T(1,128)S(1)}, u32[]{:S(2)}, u32[]{:S(2)}) collective-permute-start(f32[3,6,1,128]{3,2,1,0:T(1,128)S(1)} %get-tuple-element.68), channel_id=1, source_target_pairs={{0,1},{1,2},{2,3},{3,4},{4,5},{5,6},{6,7},{7,0},{8,9},{9,10},{10,1... | collective-permute-start | bytes 27656 | tf_op jit(solution)/shard_map/ppermute | solution.py:21
  490.1 6.8 %collective-permute-start.7 = (f32[3,6,1,128]{3,2,1,0:T(1,128)S(1)}, f32[3,6,1,128]{3,2,1,0:T(1,128)S(1)}, u32[]{:S(2)}, u32[]{:S(2)}) collective-permute-start(f32[3,6,1,128]{3,2,1,0:T(1,128)S(1)} %get-tuple-element.69), channel_id=1, source_target_pairs={{1,0},{2,1},{3,2},{4,3},{5,4},{6,5},{7,6},{0,7},{9,8},{10,9},{11,1... | collective-permute-start | bytes 27656 | tf_op jit(solution)/shard_map/ppermute | solution.py:24
  503.9 64.8 %copy-start = (f32[3,16384]{1,0:T(4,128)S(1)}, f32[3,16384]{1,0:T(4,128)}, u32[]{:S(2)}) copy-start(f32[3,16384]{1,0:T(4,128)} %param.15) | copy-start | bytes 589828
where the time goes:
time: 576 us; the launch traced here: 571 us
  other arithmetic  358 us (62%)
  local copies, waits for them, and re-layouts  165 us (29%)
  starting transfers between devices  40 us (7%)
  waiting for transfers between devices  6.46 us (1%)
    scatter-add x3, other arithmetic, deposit(): jax.ops.segment_sum(velocity_part[k] * weight, cell_ids, num_segments=cel...  257 us
    gather x1, local copies, waits for them, and re-layouts, body(): jnp.take(code_flat, cell_ids)  90.5 us
    scatter-add x1, other arithmetic, deposit(): jax.ops.segment_sum(weight, cell_ids, num_segments=cell_count)  85.8 us
    gather x2, local copies, waits for them, and re-layouts, body(): jnp.take(mean_flat, cell_ids, axis=1)  64.8 us
    ppermute x4, starting transfers between devices, with_halo(): lax.ppermute(lax.slice_in_dim(block, 0, width, axis=dim), axis, backward)  20.3 us
  transfers between devices with their start and end apart: 12, of which 2 were waited for; matrix products, arithmetic and copies ran while one was open for 17% of the time, Pallas kernels for 0%

commit v1 on v0

v1 whole, which is shorter than its diff:
```python
import functools
import math

import jax
import jax.numpy as jnp
from jax import lax
from jax.experimental import pallas as pl
from jax.experimental.pallas import tpu as pltpu
from jax.sharding import PartitionSpec as P

QUANT = 8
NFILL = 8
ANGLE = 130.0 * math.pi / 180.0

F32 = jnp.float32
BF16 = jnp.bfloat16
I32 = jnp.int32
MESH = pl.DeviceIdType.MESH

CX, CY, NZ = 4, 32, 128
HY = CY + 2
ROWS = 104
PITCH = 112
COLS = 2 * NZ
FACE = 40
NONE = PITCH - 1

STEPS = ((-1, 0), (1, 0), (0, -1), (0, 1), (-1, -1), (-1, 1), (1, -1), (1, 1))
BACK = {step: index for index, step in enumerate(STEPS)}


def split(value):
    high = value.astype(BF16)
    low = (value - high.astype(F32)).astype(BF16)
    return high, low


def kernel(
    block,
    counts, shift, pos, vel, axis, drop, out,
    acc, sums, table, code_tab, drop_tab,
    flag_x_low, flag_x_high, flag_y_low, flag_y_high,
    flag_x_got, flag_y_got, flag_d_got,
    sum_y_low, sum_y_high, sum_x_got, sum_y_got, sum_d_got,
    send_sem, recv_sem,
):
    slots = pos.shape[1]
    slabs, crosses = lax.axis_size("slab"), lax.axis_size("cross")
    me_slab, me_cross = lax.axis_index("slab"), lax.axis_index("cross")

    def place(step):
        return (
            lax.rem(me_slab + step[0] + slabs, slabs),
            lax.rem(me_cross + step[1] + crosses, crosses),
        )

    barrier = pltpu.get_barrier_semaphore()
    for step in STEPS:
        pl.semaphore_signal(barrier, inc=1, device_id=place(step), device_id_type=MESH)

    def remote(index, source, target, step):
        return pltpu.make_async_remote_copy(
            src_ref=source,
            dst_ref=target,
            send_sem=send_sem.at[index],
            recv_sem=recv_sem.at[index],
            device_id=place(step),
            device_id_type=MESH,
        )

    anchor_x = me_slab * (CX * QUANT)
    anchor_y = me_cross * (CY * QUANT)
    period_x = slabs * CX * QUANT
    period_y = crosses * CY * QUANT
    count = counts[0]
    shift_x, shift_y, shift_z = shift[0], shift[1], shift[2]

    def cells(base, lanes):
        place_x = pos[0:1, lanes] - anchor_x + QUANT
        place_y = pos[1:2, lanes] - anchor_y + QUANT
        x = ((place_x & (period_x - 1)) + shift_x) >> 3
        y = ((place_y & (period_y - 1)) + shift_y) >> 3
        z = ((pos[2:3, lanes] + shift_z) >> 3) & (NZ - 1)
        living = lax.broadcasted_iota(I32, (1, block), 1) + base < count
        row = jnp.where(living, (x >> 1) * HY + y, NONE)
        column = (x & 1) * NZ + z
        return row, column, living

    def as_bf16(value):
        return value.astype(F32).astype(BF16)

    def column_onehot(ids, column):
        return jnp.where(ids == as_bf16(column), jnp.ones((), BF16), jnp.zeros((), BF16))

    flag_x_low[0] = axis[0]
    flag_x_low[1] = drop[0]
    flag_x_high[0] = axis[CX - 1]
    flag_x_high[1] = drop[CX - 1]
    for plane in range(CX):
        flag_y_low[plane : plane + 1, :] = axis[plane, 0:1, :]
        flag_y_low[CX + plane : CX + plane + 1, :] = drop[plane, 0:1, :]
        flag_y_high[plane : plane + 1, :] = axis[plane, CY - 1 : CY, :]
        flag_y_high[CX + plane : CX + plane + 1, :] = drop[plane, CY - 1 : CY, :]

    acc[...] = jnp.zeros_like(acc)

    def deposit(index, carry):
        base = pl.multiple_of(index * block, block)
        lanes = pl.ds(base, block)
        row, column, _ = cells(base, lanes)
        high, low = split(vel[:, lanes])
        ids = as_bf16(lax.broadcasted_iota(I32, (COLS, block), 0))
        onehot = column_onehot(ids, column)
        here = ids[:PITCH] == as_bf16(row)
        nought = jnp.zeros((), BF16)
        parts = [jnp.where(here, jnp.ones((1, block), BF16), nought)]
        for k in range(3):
            for term in (high, low):
                parts.append(jnp.where(here, term[k : k + 1], nought))
        acc[...] += lax.dot_general(
            jnp.concatenate(parts, axis=0), onehot, (((1,), (1,)), ((), ())),
            preferred_element_type=F32,
        )
        return carry

    half = slots // block // 2
    lax.fori_loop(0, half, deposit, 0)

    pl.semaphore_wait(barrier, len(STEPS))
    flag_copies = []
    for index, step in enumerate(STEPS):
        if step[1] == 0:
            source = flag_x_low if step[0] < 0 else flag_x_high
            target = flag_x_got.at[index]
        else:
            source = flag_y_low if step[1] < 0 else flag_y_high
            target = flag_y_got.at[index - 2] if step[0] == 0 else flag_d_got.at[index - 4]
        copy = remote(index, source, target, step)
        copy.start()
        flag_copies.append(copy)

    lax.fori_loop(half, slots // block, deposit, 0)

    sums[0] = acc[0:ROWS, :]
    for k in range(3):
        first = (1 + 2 * k) * PITCH
        second = first + PITCH
        sums[1 + k] = acc[first : first + ROWS, :] + acc[second : second + ROWS, :]
    for pair in range(3):
        for channel in range(4):
            into = slice(2 * channel, 2 * channel + 2)
            sum_y_low[pair, into, :] = sums[channel, pair * HY : pair * HY + 2, :]
            sum_y_high[pair, into, :] = sums[channel, pair * HY + CY : pair * HY + CY + 2, :]

    sum_copies = []
    for index, step in enumerate(STEPS):
        if step[1] == 0:
            source = sums.at[:, 0:FACE, :] if step[0] < 0 else sums.at[:, ROWS - FACE : ROWS, :]
            target = sum_x_got.at[index]
        else:
            source = sum_y_low if step[1] < 0 else sum_y_high
            target = sum_y_got.at[index - 2]
            if step[0] != 0:
                source = source.at[0 if step[0] < 0 else 2]
                target = sum_d_got.at[index - 4]
        copy = remote(8 + index, source, target, step)
        copy.start()
        sum_copies.append(copy)

    code_tab[...] = jnp.zeros_like(code_tab)
    drop_tab[...] = jnp.zeros_like(drop_tab)
    for copy in flag_copies:
        copy.wait_recv()
    for plane in range(CX + 2):
        pair = plane // 2
        tile = slice(plane % 2 * NZ, plane % 2 * NZ + NZ)
        rows = slice(pair * HY + 1, pair * HY + 1 + CY)
        if plane == 0:
            side, edge = -1, CX - 1
            code_in = flag_x_got[BACK[(1, 0)], 0]
            drop_in = flag_x_got[BACK[(1, 0)], 1]
        elif plane == CX + 1:
            side, edge = 1, 0
            code_in = flag_x_got[BACK[(-1, 0)], 0]
            drop_in = flag_x_got[BACK[(-1, 0)], 1]
        else:
            side, edge = 0, plane - 1
            code_in = axis[plane - 1]
            drop_in = drop[plane - 1]
        code_tab[rows, tile] = code_in
        drop_tab[rows, tile] = drop_in
        for end in (-1, 1):
            row = pair * HY + (0 if end < 0 else HY - 1)
            index = BACK[(-side, -end)]
            got = flag_y_got.at[index - 2] if side == 0 else flag_d_got.at[index - 4]
            code_tab[row : row + 1, tile] = got[edge : edge + 1, :]
            drop_tab[row : row + 1, tile] = got[CX + edge : CX + edge + 1, :]

    for copy in sum_copies:
        copy.wait_send()
        copy.wait_recv()

    pad = FACE - HY
    low = slice(0, HY)
    high = slice(2 * HY, 3 * HY)
    off = ROWS - FACE
    for channel in range(4):
        sums[channel, low, :] += sum_x_got[BACK[(1, 0)], channel, 2 * HY - off : 3 * HY - off, :]
        sums[channel, high, :] += sum_x_got[BACK[(-1, 0)], channel, low, :]
        part = slice(2 * channel, 2 * channel + 2)
        for end in (-1, 1):
            for pair in range(3):
                first = pair * HY + (0 if end < 0 else CY)
                total = sum_y_got[BACK[(0, -end)] - 2, pair, part, :]
                if pair == 0:
                    total = total + sum_d_got[BACK[(1, -end)] - 4, part, :]
                if pair == 2:
                    total = total + sum_d_got[BACK[(-1, -end)] - 4, part, :]
                sums[channel, first : first + 2, :] += total

    fill = jnp.where(drop_tab[...] == 1, float(NFILL), 1.0)
    number = jnp.maximum(sums[0], fill)
    blank = jnp.zeros((PITCH - ROWS, COLS), F32)
    table[0:PITCH, :] = jnp.concatenate([code_tab[...].astype(F32), blank], axis=0).astype(BF16)
    for k in range(3):
        terms = split(jnp.concatenate([sums[1 + k] / number, blank], axis=0))
        for t in range(2):
            first = (1 + 2 * k + t) * PITCH
            table[first : first + PITCH, :] = terms[t]

    cosine, sine = math.cos(ANGLE), math.sin(ANGLE)

    def turn(index, carry):
        base = pl.multiple_of(index * block, block)
        lanes = pl.ds(base, block)
        row, column, living = cells(base, lanes)
        onehot = column_onehot(as_bf16(lax.broadcasted_iota(I32, (COLS, block), 0)), column)
        here = lax.broadcasted_iota(I32, (PITCH, block), 0) == row

        def pick(*channels):
            found = None
            for channel in channels:
                rows = table[channel * PITCH : (channel + 1) * PITCH, :]
                term = jnp.dot(rows, onehot, preferred_element_type=F32)
                found = term if found is None else found + term
            return jnp.sum(jnp.where(here, found, 0.0), axis=0, keepdims=True)

        code = pick(0)
        mean = [pick(1 + 2 * k, 2 + 2 * k) for k in range(3)]
        rel = [vel[k : k + 1, lanes] - mean[k] for k in range(3)]
        along_x = code < 1.5
        along_y = (code > 1.5) & (code < 3.5)
        along_z = code > 3.5
        odd = (code == 1.0) | (code == 3.0) | (code == 5.0)
        turn_by = jnp.where(odd, -sine, sine)
        plain = [cosine * r for r in rel]
        cross = [turn_by * r for r in rel]
        new_x = jnp.where(along_x, rel[0], plain[0] + jnp.where(along_y, cross[2], -cross[1]))
        new_y = jnp.where(along_y, rel[1], plain[1] + jnp.where(along_x, -cross[2], cross[0]))
        new_z = jnp.where(along_z, rel[2], plain[2] + jnp.where(along_x, cross[1], -cross[0]))
        for k, new in enumerate((new_x, new_y, new_z)):
            out[k : k + 1, lanes] = jnp.where(living, mean[k] + new, 0.0)
        return carry

    lax.fori_loop(0, slots // block, turn, 0)

    for copy in flag_copies:
        copy.wait_send()


def body(positions, velocities, counts, grid_shift, axis_index, droplet):
    smem = pl.BlockSpec(memory_space=pltpu.SMEM)
    vmem = pl.BlockSpec(memory_space=pltpu.VMEM)
    block = 2048
    return pl.pallas_call(
        functools.partial(kernel, block),
        out_shape=jax.ShapeDtypeStruct(velocities.shape, F32),
        in_specs=[smem, smem, vmem, vmem, vmem, vmem],
        out_specs=vmem,
        scratch_shapes=[
            pltpu.VMEM((7 * PITCH, COLS), F32),
            pltpu.VMEM((4, ROWS, COLS), F32),
            pltpu.VMEM((7 * PITCH, COLS), BF16),
            pltpu.VMEM((ROWS, COLS), I32),
            pltpu.VMEM((ROWS, COLS), I32),
            pltpu.VMEM((2, CY, NZ), I32),
            pltpu.VMEM((2, CY, NZ), I32),
            pltpu.VMEM((2 * CX, NZ), I32),
            pltpu.VMEM((2 * CX, NZ), I32),
            pltpu.VMEM((2, 2, CY, NZ), I32),
            pltpu.VMEM((2, 2 * CX, NZ), I32),
            pltpu.VMEM((4, 2 * CX, NZ), I32),
            pltpu.VMEM((3, 8, COLS), F32),
            pltpu.VMEM((3, 8, COLS), F32),
            pltpu.VMEM((2, 4, FACE, COLS), F32),
            pltpu.VMEM((2, 3, 8, COLS), F32),
            pltpu.VMEM((4, 8, COLS), F32),
            pltpu.SemaphoreType.DMA((16,)),
            pltpu.SemaphoreType.DMA((16,)),
        ],
        compiler_params=pltpu.CompilerParams(
            collective_id=0, has_side_effects=True, vmem_limit_bytes=48 << 20
        ),
        name="collision_step",
    )(counts, grid_shift, positions, velocities, axis_index, droplet)


def solution(mesh):
    placed = (
        P(None, ("slab", "cross")),
        P(None, ("slab", "cross")),
        P(("slab", "cross")),
        P(),
        P("slab", "cross", None),
        P("slab", "cross", None),
    )
    return jax.shard_map(
        body, mesh=mesh, in_specs=placed, out_specs=P(None, ("slab", "cross")), check_vma=False
    )
```

time: 576 us -> 41.2 us (0.07)
  the two profiles are of different devices: /device:TPU:448 before, /device:TPU:6 now
where the time goes in v1:
time: 41.2 us; the launch traced here: 40.9 us
  Pallas kernels  35.9 us (87%)
  local copies, waits for them, and re-layouts  4.28 us (10%)
  between operations  0.69 us (2%)
    pallas_call x1, Pallas kernels, body(): pl.pallas_call(functools.partial(kernel, block), out_shape=jax.ShapeDtype...  35.9 us
    unnamed x11, local copies, waits for them, and re-layouts  4.28 us

profile of v1, /device:TPU:6, one launch (start us, length us, event | category | flops | bytes accessed | tf_op | source)
XLA Modules:
  0.0 40.9 jit_solution(3997098653684796377)
XLA Ops:
  0.0 0.0 copy-start.4
  0.7 0.0 copy-done.4
  0.7 0.0 copy-start
  0.7 0.9 %copy-done = s32[3,16384]{1,0:T(4,128)S(1)} copy-done((s32[3,16384]{1,0:T(4,128)S(1)}, s32[3,16384]{1,0:T(4,128)}, u32[]{:S(2)}) %copy-start) | copy-done | bytes 196632
  1.6 0.0 copy-start.1
  1.6 0.9 %copy-done.1 = f32[3,16384]{1,0:T(4,128)S(1)} copy-done((f32[3,16384]{1,0:T(4,128)S(1)}, f32[3,16384]{1,0:T(4,128)}, u32[]{:S(2)}) %copy-start.1) | copy-done | bytes 196632
  2.6 0.0 copy-start.2
  2.6 0.8 %copy-done.2 = s32[4,32,128]{2,1,0:T(8,128)S(1)} copy-done((s32[4,32,128]{2,1,0:T(8,128)S(1)}, s32[4,32,128]{2,1,0:T(8,128)}, u32[]{:S(2)}) %copy-start.2) | copy-done | bytes 65560
  3.4 0.0 copy-start.3
  3.4 0.8 %copy-done.3 = s32[4,32,128]{2,1,0:T(8,128)S(1)} copy-done((s32[4,32,128]{2,1,0:T(8,128)S(1)}, s32[4,32,128]{2,1,0:T(8,128)}, u32[]{:S(2)}) %copy-start.3) | copy-done | bytes 65560
  4.3 35.9 %collision_step.1 = f32[3,16384]{1,0:T(4,128)S(1)} custom-call(s32[1]{0:T(128)S(6)} %copy.8.counts, s32[3]{0:T(128)S(1)} %copy-done.4, s32[3,16384]{1,0:T(4,128)S(1)} %copy-done, f32[3,16384]{1,0:T(4,128)S(1)} %copy-done.1, s32[4,32,128]{2,1,0:T(8,128)S(1)} %copy-done.2, s32[4,32,128]{2,1,0:T(8,128)S(1)} %copy-done.3), custom_call_target="tpu_custom_call" | custom-call | tf_op jit(solution)/shard_map/collision_step/pallas_call | solution.py:275
  40.2 0.7 %copy.9 = f32[3,16384]{1,0:T(4,128)} copy(f32[3,16384]{1,0:T(4,128)S(1)} %collision_step.1) | data formatting | bytes 393216
Async XLA Ops:
  0.0 0.7 %copy-start.4 = (s32[3]{0:T(128)S(1)}, s32[3]{0:T(128)}, u32[]{:S(2)}) copy-start(s32[3]{0:T(128)} %shift.1) | copy-start | bytes 40
  0.7 1.0 %copy-start = (s32[3,16384]{1,0:T(4,128)S(1)}, s32[3,16384]{1,0:T(4,128)}, u32[]{:S(2)}) copy-start(s32[3,16384]{1,0:T(4,128)} %pos.1) | copy-start | bytes 589828
  1.6 0.9 %copy-start.1 = (f32[3,16384]{1,0:T(4,128)S(1)}, f32[3,16384]{1,0:T(4,128)}, u32[]{:S(2)}) copy-start(f32[3,16384]{1,0:T(4,128)} %vel.1) | copy-start | bytes 589828
  2.6 0.8 %copy-start.2 = (s32[4,32,128]{2,1,0:T(8,128)S(1)}, s32[4,32,128]{2,1,0:T(8,128)}, u32[]{:S(2)}) copy-start(s32[4,32,128]{2,1,0:T(8,128)} %axis.1) | copy-start | bytes 196612
  3.4 0.8 %copy-start.3 = (s32[4,32,128]{2,1,0:T(8,128)S(1)}, s32[4,32,128]{2,1,0:T(8,128)}, u32[]{:S(2)}) copy-start(s32[4,32,128]{2,1,0:T(8,128)} %drop.1) | copy-start | bytes 196612

commit v2 on v1

v2 whole, which is shorter than its diff:
```python
import functools
import math

import jax
import jax.numpy as jnp
from jax import lax
from jax.experimental import pallas as pl
from jax.experimental.pallas import tpu as pltpu
from jax.sharding import PartitionSpec as P

QUANT = 8
NFILL = 8
ANGLE = 130.0 * math.pi / 180.0

F32 = jnp.float32
BF16 = jnp.bfloat16
I32 = jnp.int32
MESH = pl.DeviceIdType.MESH

CX, CY, NZ = 4, 32, 128
COLS = 2 * NZ
OUTER, EDGE, INNER = 64, 16, 32
EDGE_AT = OUTER
INNER_AT = OUTER + EDGE
NONE = 127
FIRST = OUTER + EDGE
HALF = OUTER // 2
MID = CY - 2

STEPS = ((-1, 0), (1, 0), (0, -1), (0, 1), (-1, -1), (-1, 1), (1, -1), (1, 1))
SENT_BY = {step: index for index, step in enumerate(STEPS)}


def split(value):
    high = value.astype(BF16)
    low = (value - high.astype(F32)).astype(BF16)
    return high, low


def as_bf16(value):
    return value.astype(F32).astype(BF16)


def kernel(
    block,
    counts_in, shift_in, pos_in, vel_in, axis_in, drop_in, out,
    counts, shift, pos, vel, axis, drop, load_sem,
    rows, onehots, picked,
    acc_first, acc_inner, sum_outer, sum_inner, sum_edge, part_edge,
    table_outer, table_inner, table_edge,
    code_outer, drop_outer, code_inner, drop_inner, code_edge, drop_edge,
    flag_x_low, flag_x_high, flag_y_low, flag_y_high,
    flag_x_got, flag_y_got, flag_d_got,
    outer_got, edge_x_got, edge_y_got, edge_d_got,
    send_sem, recv_sem,
):
    slots = pos.shape[1]
    slabs, crosses = lax.axis_size("slab"), lax.axis_size("cross")
    me_slab, me_cross = lax.axis_index("slab"), lax.axis_index("cross")

    def place(step):
        return (
            lax.rem(me_slab + step[0] + slabs, slabs),
            lax.rem(me_cross + step[1] + crosses, crosses),
        )

    barrier = pltpu.get_barrier_semaphore()
    for step in STEPS:
        pl.semaphore_signal(barrier, inc=1, device_id=place(step), device_id_type=MESH)

    loads = [
        pltpu.make_async_copy(source, target, load_sem.at[index])
        for index, (source, target) in enumerate((
            (counts_in, counts), (shift_in, shift), (pos_in, pos),
            (vel_in, vel), (axis_in, axis), (drop_in, drop),
        ))
    ]
    for load in loads:
        load.start()

    def remote(index, source, target, step):
        return pltpu.make_async_remote_copy(
            src_ref=source,
            dst_ref=target,
            send_sem=send_sem.at[index],
            recv_sem=recv_sem.at[index],
            device_id=place(step),
            device_id_type=MESH,
        )

    def for_blocks(step):
        if slots == block:
            step(0)
        else:
            def run(index, carry):
                step(pl.multiple_of(index * block, block))
                return carry

            lax.fori_loop(0, slots // block, run, 0)

    acc_first[...] = jnp.zeros_like(acc_first)
    acc_inner[...] = jnp.zeros_like(acc_inner)
    for ref in (code_outer, drop_outer, code_inner, drop_inner, code_edge, drop_edge, sum_edge):
        ref[...] = jnp.zeros_like(ref)

    for load in loads[:4]:
        load.wait()
    anchor_x = me_slab * (CX * QUANT)
    anchor_y = me_cross * (CY * QUANT)
    period_x = slabs * CX * QUANT
    period_y = crosses * CY * QUANT
    count = counts[0]
    shift_x, shift_y, shift_z = shift[0], shift[1], shift[2]

    def find(base):
        lanes = pl.ds(base, block)
        place_x = pos[0:1, lanes] - anchor_x + QUANT
        place_y = pos[1:2, lanes] - anchor_y + QUANT
        x = ((place_x & (period_x - 1)) + shift_x) >> 3
        y = ((place_y & (period_y - 1)) + shift_y) >> 3
        z = ((pos[2:3, lanes] + shift_z) >> 3) & (NZ - 1)
        pair = x >> 1
        first = jnp.where(pair == 1, INNER_AT - 2, pair * (HALF // 2) - 2)
        at_low, at_high = y < 2, y >= CY
        row = jnp.where(at_low | at_high, EDGE_AT + pair * 4 + jnp.where(at_high, -MID, 0), first) + y
        living = lax.broadcasted_iota(I32, (1, block), 1) + base < count
        row = jnp.where(living, row, NONE)
        rows[:, lanes] = row
        column = as_bf16((x & 1) * NZ + z)
        ids = as_bf16(lax.broadcasted_iota(I32, (COLS, block), 0))
        onehot = jnp.where(ids == column, jnp.ones((), BF16), jnp.zeros((), BF16))
        onehots[:, lanes] = onehot
        return row, onehot

    def deposit(acc, first, pitch, base):
        lanes = pl.ds(base, block)
        if first == 0:
            row, onehot = find(base)
        else:
            row, onehot = rows[:, lanes], onehots[:, lanes]
        high, low = split(vel[:, lanes])
        ids = as_bf16(lax.broadcasted_iota(I32, (pitch, block), 0) + first)
        here = ids == as_bf16(row)
        nought = jnp.zeros((), BF16)
        parts = [jnp.where(here, jnp.ones((1, block), BF16), nought)]
        for k in range(3):
            for term in (high, low):
                parts.append(jnp.where(here, term[k : k + 1], nought))
        acc[...] += lax.dot_general(
            jnp.concatenate(parts, axis=0), onehot, (((1,), (1,)), ((), ())),
            preferred_element_type=F32,
        )

    def total(acc, pitch, channel, first, size):
        if channel == 0:
            return acc[first : first + size, :]
        high = (2 * channel - 1) * pitch + first
        low = high + pitch
        return acc[high : high + size, :] + acc[low : low + size, :]

    for_blocks(functools.partial(deposit, acc_first, 0, FIRST))

    for channel in range(4):
        sum_outer[channel] = total(acc_first, FIRST, channel, 0, OUTER)
        edge = total(acc_first, FIRST, channel, EDGE_AT, EDGE)
        for pair in range(3):
            for side in range(2):
                at = side * 8 + channel * 2
                part_edge[pair, at : at + 2, :] = edge[pair * 4 + side * 2 : pair * 4 + side * 2 + 2, :]
    for load in loads[4:]:
        load.wait()
    flag_x_low[0] = axis[0]
    flag_x_low[1] = drop[0]
    flag_x_high[0] = axis[CX - 1]
    flag_x_high[1] = drop[CX - 1]
    for plane in range(CX):
        flag_y_low[plane : plane + 1, :] = axis[plane, 0:1, :]
        flag_y_low[CX + plane : CX + plane + 1, :] = drop[plane, 0:1, :]
        flag_y_high[plane : plane + 1, :] = axis[plane, CY - 1 : CY, :]
        flag_y_high[CX + plane : CX + plane + 1, :] = drop[plane, CY - 1 : CY, :]

    pl.semaphore_wait(barrier, len(STEPS))

    x_copies = []
    for index, step in enumerate(STEPS[:2]):
        half = slice(0, HALF) if step[0] < 0 else slice(HALF, OUTER)
        x_copies.append(remote(16 + index, sum_outer.at[:, half, :], outer_got.at[index], step))
        source = flag_x_low if step[0] < 0 else flag_x_high
        x_copies.append(remote(index, source, flag_x_got.at[index], step))
    edge_copies = []
    for index, step in enumerate(STEPS):
        ends = slice(0, 16) if step[1] == 0 else slice(0, 8) if step[1] < 0 else slice(8, 16)
        if step[0] == 0:
            source, target = part_edge.at[:, ends, :], edge_y_got.at[index - 2]
        else:
            source = part_edge.at[0 if step[0] < 0 else 2, ends, :]
            target = edge_x_got.at[index] if step[1] == 0 else edge_d_got.at[index - 4]
        edge_copies.append(remote(8 + index, source, target, step))
        if step[1] != 0:
            source = flag_y_low if step[1] < 0 else flag_y_high
            target = flag_y_got.at[index - 2] if step[0] == 0 else flag_d_got.at[index - 4]
            edge_copies.append(remote(index, source, target, step))
    for copy in x_copies + edge_copies:
        copy.start()

    def fill_table(table, pitch, sums, code, wall):
        number = jnp.maximum(sums[0], jnp.where(wall[...] == 1, float(NFILL), 1.0))
        for k in range(3):
            high, low = split(sums[1 + k] / number)
            table[k * pitch : (k + 1) * pitch, :] = high
            table[(4 + k) * pitch : (5 + k) * pitch, :] = low
        table[3 * pitch : 4 * pitch, :] = as_bf16(code[...])

    def pick(table, pitch, first, base):
        lanes = pl.ds(base, block)
        onehot = onehots[:, lanes]
        here = lax.broadcasted_iota(I32, (pitch, block), 0) + first == rows[:, lanes]
        highs = jnp.dot(table[0 : 4 * pitch, :], onehot, preferred_element_type=F32)
        lows = jnp.dot(table[4 * pitch : 7 * pitch, :], onehot, preferred_element_type=F32)
        found = []
        for k in range(4):
            part = highs[k * pitch : (k + 1) * pitch]
            if k < 3:
                part = part + lows[k * pitch : (k + 1) * pitch]
            found.append(jnp.sum(jnp.where(here, part, 0.0), axis=0, keepdims=True))
        return found

    for_blocks(functools.partial(deposit, acc_inner, INNER_AT, INNER))
    for channel in range(4):
        sum_inner[channel] = total(acc_inner, INNER, channel, 0, INNER)
    for tile in range(2):
        lanes = slice(tile * NZ, (tile + 1) * NZ)
        code_inner[0:MID, lanes] = axis[1 + tile, 1 : CY - 1, :]
        drop_inner[0:MID, lanes] = drop[1 + tile, 1 : CY - 1, :]
    fill_table(table_inner, INNER, sum_inner, code_inner, drop_inner)

    def pick_inner(base):
        for k, found in enumerate(pick(table_inner, INNER, INNER_AT, base)):
            picked[k : k + 1, pl.ds(base, block)] = found

    for_blocks(pick_inner)

    from_left, from_right = SENT_BY[(1, 0)], SENT_BY[(-1, 0)]
    for copy in x_copies:
        copy.wait_recv()
    for flag, (own, code) in enumerate(((axis, code_outer), (drop, drop_outer))):
        code[0:MID, 0:NZ] = flag_x_got[from_left, flag, 1 : CY - 1, :]
        code[0:MID, NZ:COLS] = own[0, 1 : CY - 1, :]
        code[HALF : HALF + MID, 0:NZ] = own[CX - 1, 1 : CY - 1, :]
        code[HALF : HALF + MID, NZ:COLS] = flag_x_got[from_right, flag, 1 : CY - 1, :]
    both = [
        jnp.concatenate(
            [
                sum_outer[channel, 0:HALF, :] + outer_got[from_left, channel],
                sum_outer[channel, HALF:OUTER, :] + outer_got[from_right, channel],
            ],
            axis=0,
        )
        for channel in range(4)
    ]
    fill_table(table_outer, OUTER, both, code_outer, drop_outer)

    def pick_outer(base):
        for k, found in enumerate(pick(table_outer, OUTER, 0, base)):
            picked[k : k + 1, pl.ds(base, block)] += found

    for_blocks(pick_outer)

    for copy in edge_copies:
        copy.wait_recv()
    for pair in range(3):
        for side, end in enumerate((-1, 1)):
            ends = slice(side * 8, side * 8 + 8)
            whole = part_edge[pair, ends, :] + edge_y_got[SENT_BY[(0, -end)] - 2, pair]
            if pair != 1:
                step = 1 if pair == 0 else -1
                whole = whole + edge_x_got[SENT_BY[(step, 0)], ends, :]
                whole = whole + edge_d_got[SENT_BY[(step, -end)] - 4]
            for channel in range(4):
                at = pair * 4 + side * 2
                sum_edge[channel, at : at + 2, :] = whole[2 * channel : 2 * channel + 2]
            for tile in range(2):
                plane = 2 * pair + tile
                lanes = slice(tile * NZ, (tile + 1) * NZ)
                beyond = -1 if plane == 0 else 1 if plane == CX + 1 else 0
                last = CX - 1 if plane == 0 else 0 if plane == CX + 1 else plane - 1
                inside = 0 if side == 0 else CY - 1
                halo = flag_y_got.at[SENT_BY[(0, -end)] - 2]
                if beyond != 0:
                    halo = flag_d_got.at[SENT_BY[(-beyond, -end)] - 4]
                near = pair * 4 + (1 if side == 0 else 2)
                far = pair * 4 + (0 if side == 0 else 3)
                for flag, (own, code) in enumerate(((axis, code_edge), (drop, drop_edge))):
                    if beyond == 0:
                        value = own[last, inside : inside + 1, :]
                    else:
                        value = flag_x_got[SENT_BY[(-beyond, 0)], flag, inside : inside + 1, :]
                    code[near : near + 1, lanes] = value
                    code[far : far + 1, lanes] = halo[flag * CX + last : flag * CX + last + 1, :]
    fill_table(table_edge, EDGE, sum_edge, code_edge, drop_edge)

    cosine, sine = math.cos(ANGLE), math.sin(ANGLE)

    def finish(base):
        lanes = pl.ds(base, block)
        found = pick(table_edge, EDGE, EDGE_AT, base)
        mean = [picked[k : k + 1, lanes] + found[k] for k in range(3)]
        code = picked[3:4, lanes] + found[3]
        rel = [vel[k : k + 1, lanes] - mean[k] for k in range(3)]
        along_x = code < 1.5
        along_y = (code > 1.5) & (code < 3.5)
        along_z = code > 3.5
        odd = (code == 1.0) | (code == 3.0) | (code == 5.0)
        turn_by = jnp.where(odd, -sine, sine)
        plain = [cosine * r for r in rel]
        cross = [turn_by * r for r in rel]
        new_x = jnp.where(along_x, rel[0], plain[0] + jnp.where(along_y, cross[2], -cross[1]))
        new_y = jnp.where(along_y, rel[1], plain[1] + jnp.where(along_x, -cross[2], cross[0]))
        new_z = jnp.where(along_z, rel[2], plain[2] + jnp.where(along_x, cross[1], -cross[0]))
        living = rows[:, lanes] != NONE
        for k, new in enumerate((new_x, new_y, new_z)):
            out[k : k + 1, lanes] = jnp.where(living, mean[k] + new, 0.0)

    for_blocks(finish)

    for copy in x_copies + edge_copies:
        copy.wait_send()


def body(positions, velocities, counts, grid_shift, axis_index, droplet):
    hbm = pl.BlockSpec(memory_space=pl.ANY)
    slots = positions.shape[1]
    block = BLOCK
    cells = (CX, CY, NZ)
    vmem = pltpu.VMEM
    return pl.pallas_call(
        functools.partial(kernel, block),
        out_shape=jax.ShapeDtypeStruct(velocities.shape, F32),
        in_specs=[hbm] * 6,
        out_specs=pl.BlockSpec(memory_space=pltpu.VMEM),
        scratch_shapes=[
            pltpu.SMEM((1,), I32), pltpu.SMEM((3,), I32),
            vmem((3, slots), I32), vmem((3, slots), F32), vmem(cells, I32), vmem(cells, I32),
            pltpu.SemaphoreType.DMA((6,)),
            vmem((1, slots), I32), vmem((COLS, slots), BF16), vmem((4, slots), F32),
            vmem((7 * FIRST, COLS), F32), vmem((7 * INNER, COLS), F32),
            vmem((4, OUTER, COLS), F32), vmem((4, INNER, COLS), F32), vmem((4, EDGE, COLS), F32),
            vmem((3, 16, COLS), F32),
            vmem((7 * OUTER, COLS), BF16), vmem((7 * INNER, COLS), BF16), vmem((7 * EDGE, COLS), BF16),
            vmem((OUTER, COLS), I32), vmem((OUTER, COLS), I32),
            vmem((INNER, COLS), I32), vmem((INNER, COLS), I32),
            vmem((EDGE, COLS), I32), vmem((EDGE, COLS), I32),
            vmem((2, CY, NZ), I32), vmem((2, CY, NZ), I32),
            vmem((2 * CX, NZ), I32), vmem((2 * CX, NZ), I32),
            vmem((2, 2, CY, NZ), I32), vmem((2, 2 * CX, NZ), I32), vmem((4, 2 * CX, NZ), I32),
            vmem((2, 4, HALF, COLS), F32), vmem((2, 16, COLS), F32),
            vmem((2, 3, 8, COLS), F32), vmem((4, 8, COLS), F32),
            pltpu.SemaphoreType.DMA((18,)),
            pltpu.SemaphoreType.DMA((18,)),
        ],
        compiler_params=pltpu.CompilerParams(
            collective_id=0, has_side_effects=True, vmem_limit_bytes=VMEM_MIB << 20
        ),
        name="collision_step",
    )(counts, grid_shift, positions, velocities, axis_index, droplet)


BLOCK = 8192
VMEM_MIB = 58


def solution(mesh):
    placed = (
        P(None, ("slab", "cross")),
        P(None, ("slab", "cross")),
        P(("slab", "cross")),
        P(),
        P("slab", "cross", None),
        P("slab", "cross", None),
    )
    return jax.shard_map(
        body, mesh=mesh, in_specs=placed, out_specs=P(None, ("slab", "cross")), check_vma=False
    )
```

time: 41.2 us -> 29.5 us (0.72)
  Pallas kernels: 35.9 us -> 27 us
  local copies, waits for them, and re-layouts: 4.28 us -> 1.7 us
    pallas_call x1, Pallas kernels: 35.9 us -> 27 us  [body(): pl.pallas_call(functools.partial(kernel, block), out_shape=jax.ShapeDtype...]
    unnamed x11 -> x1, local copies, waits for them, and re-layouts: 4.28 us -> 1.7 us
where the time goes in v2:
time: 29.5 us; the launch traced here: 29.4 us
  Pallas kernels  27 us (92%)
  local copies, waits for them, and re-layouts  1.7 us (6%)
  between operations  0.66 us (2%)
    pallas_call x1, Pallas kernels, body(): pl.pallas_call(functools.partial(kernel, block), out_shape=jax.ShapeDtype...  27 us
    unnamed x1, local copies, waits for them, and re-layouts  1.7 us

profile of v2, /device:TPU:6, one launch (start us, length us, event | category | flops | bytes accessed | tf_op | source)
XLA Modules:
  0.0 29.4 jit_solution(17375572986730608281)
XLA Ops:
  0.7 27.0 %collision_step.1 = f32[3,16384]{1,0:T(4,128)} custom-call(s32[1]{0:T(128)S(6)} %copy.8.counts_in, s32[3]{0:T(128)} %shift_in.1, s32[3,16384]{1,0:T(4,128)} %pos_in.1, f32[3,16384]{1,0:T(4,128)} %vel_in.1, s32[4,32,128]{2,1,0:T(8,128)} %axis_in.1, s32[4,32,128]{2,1,0:T(8,128)} %drop_in.1), custom_call_target="tpu_custom_call" | custom-call | tf_op jit(solution)/shard_map/collision_step/pallas_call | solution.py:336
  27.7 1.7 %copy.9 = f32[3,16384]{1,0:T(4,128)} copy(f32[3,16384]{1,0:T(4,128)} %collision_step.1) | data formatting | bytes 393216

commit v3 on v2

v3 whole, which is shorter than its diff:
```python
import functools
import math

import jax
import jax.numpy as jnp
from jax import lax
from jax.experimental import pallas as pl
from jax.experimental.pallas import tpu as pltpu
from jax.sharding import PartitionSpec as P

QUANT = 8
NFILL = 8
ANGLE = 130.0 * math.pi / 180.0

F32 = jnp.float32
BF16 = jnp.bfloat16
I32 = jnp.int32
MESH = pl.DeviceIdType.MESH

CX, CY, NZ = 4, 32, 128
COLS = 2 * NZ
OUTER, EDGE, INNER = 64, 16, 32
EDGE_AT = OUTER
INNER_AT = OUTER + EDGE
FIRST = OUTER + EDGE
NONE = 127
HALF = OUTER // 2
MID = CY - 2

STEPS = ((-1, 0), (1, 0), (0, -1), (0, 1), (-1, -1), (-1, 1), (1, -1), (1, 1))
SENT_BY = {step: index for index, step in enumerate(STEPS)}


def split(value):
    high = value.astype(BF16)
    low = (value - high.astype(F32)).astype(BF16)
    return high, low


def as_bf16(value):
    return value.astype(F32).astype(BF16)


def kernel(
    block,
    counts_in, shift_in, pos_in, vel_in, axis_in, drop_in, out_hbm,
    counts, shift, pos_x, pos_y, pos_z, vel_x, vel_y, vel_z, axis, drop, out_x, out_y, out_z, load_sem,
    rows, onehots, mean_x, mean_y, mean_z, codes,
    acc_first, acc_inner, sum_outer, sum_inner, sum_edge, part_edge,
    table_outer, table_inner, table_edge,
    code_outer, drop_outer, code_inner, drop_inner, code_edge, drop_edge,
    flag_x_low, flag_x_high, flag_y_low, flag_y_high,
    flag_x_got, flag_y_got, flag_d_got,
    outer_got, edge_x_got, edge_y_got, edge_d_got,
    send_sem, recv_sem, late_sem,
):
    slots = rows.shape[1]
    vel = (vel_x, vel_y, vel_z)
    outs = (out_x, out_y, out_z)
    picked = (mean_x, mean_y, mean_z, codes)
    slabs, crosses = lax.axis_size("slab"), lax.axis_size("cross")
    me_slab, me_cross = lax.axis_index("slab"), lax.axis_index("cross")

    def place(step):
        return (
            lax.rem(me_slab + step[0] + slabs, slabs),
            lax.rem(me_cross + step[1] + crosses, crosses),
        )

    first_in = me_cross == 0
    last_in = me_cross == crosses - 1

    def greet(semaphore, ends):
        for step in STEPS:
            if step[1] in ends:
                pl.semaphore_signal(semaphore, inc=1, device_id=place(step), device_id_type=MESH)

    barrier = pltpu.get_barrier_semaphore()
    greet(barrier, (-1, 0))
    pl.when(jnp.logical_not(last_in))(lambda: greet(barrier, (1,)))

    loads = [
        pltpu.make_async_copy(source, target, load_sem.at[index])
        for index, (source, target) in enumerate((
            (counts_in, counts), (shift_in, shift),
            (pos_in.at[0:1, :], pos_x), (pos_in.at[1:2, :], pos_y), (pos_in.at[2:3, :], pos_z),
            (vel_in.at[0:1, :], vel_x), (vel_in.at[1:2, :], vel_y), (vel_in.at[2:3, :], vel_z),
            (axis_in, axis), (drop_in, drop),
        ))
    ]
    for load in loads:
        load.start()

    def remote(index, source, target, step):
        return pltpu.make_async_remote_copy(
            src_ref=source,
            dst_ref=target,
            send_sem=send_sem.at[index],
            recv_sem=recv_sem.at[index],
            device_id=place(step),
            device_id_type=MESH,
        )

    def for_blocks(step, size):
        def run(index, carry):
            step(pl.multiple_of(index * size, size), size)
            return carry

        lax.fori_loop(0, slots // size, run, 0)

    acc_first[...] = jnp.zeros_like(acc_first)
    acc_inner[...] = jnp.zeros_like(acc_inner)
    for ref in (code_outer, drop_outer, code_inner, drop_inner, code_edge, drop_edge, sum_edge):
        ref[...] = jnp.zeros_like(ref)

    anchor_x = me_slab * (CX * QUANT)
    anchor_y = me_cross * (CY * QUANT)
    period_x = slabs * CX * QUANT
    period_y = crosses * CY * QUANT
    for load in loads[:8]:
        load.wait()
    count = counts[0, 0]
    shift_x, shift_y, shift_z = shift[0], shift[1], shift[2]

    def find(base, size):
        lanes = pl.ds(base, size)
        x = (((pos_x[:, lanes] - anchor_x + QUANT) & (period_x - 1)) + shift_x) >> 3
        y = (((pos_y[:, lanes] - anchor_y + QUANT) & (period_y - 1)) + shift_y) >> 3
        z = ((pos_z[:, lanes] + shift_z) >> 3) & (NZ - 1)
        pair = x >> 1
        at_low, at_high = y < 2, y >= CY
        edge = pair * 4 + jnp.where(at_high, EDGE_AT - MID, EDGE_AT)
        other = jnp.where(pair == 1, INNER_AT - 2, pair * (HALF // 2) - 2)
        row = jnp.where(at_low | at_high, edge, other) + y
        living = lax.broadcasted_iota(I32, (1, size), 1) + base < count
        row = jnp.where(living, row, NONE)
        rows[:, lanes] = row
        column = as_bf16((x & 1) * NZ + z)
        ids = as_bf16(lax.broadcasted_iota(I32, (COLS, size), 0))
        onehot = jnp.where(ids == column, jnp.ones((), BF16), jnp.zeros((), BF16))
        onehots[:, lanes] = onehot
        return row, onehot

    def deposit(acc, first, pitch, base, size):
        lanes = pl.ds(base, size)
        if first == 0:
            row, onehot = find(base, size)
        else:
            row, onehot = rows[:, lanes], onehots[:, lanes]
        ids = as_bf16(lax.broadcasted_iota(I32, (pitch, size), 0) + first)
        here = ids == as_bf16(row)
        nought = jnp.zeros((), BF16)
        parts = [jnp.where(here, jnp.ones((1, size), BF16), nought)]
        for k in range(3):
            for term in split(vel[k][:, lanes]):
                parts.append(jnp.where(here, term, nought))
        acc[...] += lax.dot_general(
            jnp.concatenate(parts, axis=0), onehot, (((1,), (1,)), ((), ())),
            preferred_element_type=F32,
        )

    def total(acc, pitch, channel, first, size):
        if channel == 0:
            return acc[first : first + size, :]
        high = (2 * channel - 1) * pitch + first
        low = high + pitch
        return acc[high : high + size, :] + acc[low : low + size, :]

    def fill_table(table, pitch, sums, code, wall):
        number = jnp.maximum(sums[0], jnp.where(wall[...] == 1, float(NFILL), 1.0))
        for k in range(3):
            high, low = split(sums[1 + k] / number)
            table[k * pitch : (k + 1) * pitch, :] = high
            table[(4 + k) * pitch : (5 + k) * pitch, :] = low
        table[3 * pitch : 4 * pitch, :] = as_bf16(code[...])

    def pick(table, pitch, first, base, size):
        lanes = pl.ds(base, size)
        onehot = onehots[:, lanes]
        here = lax.broadcasted_iota(I32, (pitch, size), 0) + first == rows[:, lanes]
        terms = jnp.dot(table[...], onehot, preferred_element_type=F32)
        found = []
        for k in range(4):
            part = terms[k * pitch : (k + 1) * pitch]
            if k < 3:
                part = part + terms[(4 + k) * pitch : (5 + k) * pitch]
            found.append(jnp.sum(jnp.where(here, part, 0.0), axis=0, keepdims=True))
        return found

    x_copies, edge_copies, down_copies = [], [], []
    for index, step in enumerate(STEPS[:2]):
        half = slice(0, HALF) if step[0] < 0 else slice(HALF, OUTER)
        x_copies.append(remote(16 + index, sum_outer.at[:, half, :], outer_got.at[index], step))
        source = flag_x_low if step[0] < 0 else flag_x_high
        x_copies.append(remote(index, source, flag_x_got.at[index], step))
    for index, step in sorted(enumerate(STEPS), key=lambda entry: -entry[1][1]):
        ends = slice(0, 16) if step[1] == 0 else slice(0, 8) if step[1] < 0 else slice(8, 16)
        if step[0] == 0:
            source, target = part_edge.at[:, ends, :], edge_y_got.at[index - 2]
        else:
            source = part_edge.at[0 if step[0] < 0 else 2, ends, :]
            target = edge_x_got.at[index] if step[1] == 0 else edge_d_got.at[index - 4]
        into = down_copies if step[1] < 0 else edge_copies
        into.append(remote(8 + index, source, target, step))
        if step[1] != 0:
            source = flag_y_low if step[1] < 0 else flag_y_high
            target = flag_y_got.at[index - 2] if step[0] == 0 else flag_d_got.at[index - 4]
            into.append(remote(index, source, target, step))

    def start_down():
        for copy in down_copies:
            copy.start()

    def start_late():
        pl.semaphore_wait(late_sem, 3)
        start_down()

    for_blocks(functools.partial(deposit, acc_first, 0, FIRST), block[0])
    for channel in range(4):
        sum_outer[channel] = total(acc_first, FIRST, channel, 0, OUTER)
        edge = total(acc_first, FIRST, channel, EDGE_AT, EDGE)
        for pair in range(3):
            for side in range(2):
                at = side * 8 + channel * 2
                part_edge[pair, at : at + 2, :] = edge[pair * 4 + side * 2 : pair * 4 + side * 2 + 2, :]
    for load in loads[8:]:
        load.wait()
    flag_x_low[0] = axis[0]
    flag_x_low[1] = drop[0]
    flag_x_high[0] = axis[CX - 1]
    flag_x_high[1] = drop[CX - 1]
    for plane in range(CX):
        flag_y_low[plane : plane + 1, :] = axis[plane, 0:1, :]
        flag_y_low[CX + plane : CX + plane + 1, :] = drop[plane, 0:1, :]
        flag_y_high[plane : plane + 1, :] = axis[plane, CY - 1 : CY, :]
        flag_y_high[CX + plane : CX + plane + 1, :] = drop[plane, CY - 1 : CY, :]

    pl.semaphore_wait(barrier, jnp.where(first_in, len(STEPS) - 3, len(STEPS)))
    for copy in edge_copies:
        copy.start()
    pl.when(jnp.logical_not(first_in))(start_down)
    for copy in x_copies:
        copy.start()
    pl.when(last_in)(lambda: greet(late_sem, (1,)))

    for_blocks(functools.partial(deposit, acc_inner, INNER_AT, INNER), block[1])
    for channel in range(4):
        sum_inner[channel] = total(acc_inner, INNER, channel, 0, INNER)

    for tile in range(2):
        lanes = slice(tile * NZ, (tile + 1) * NZ)
        code_inner[0:MID, lanes] = axis[1 + tile, 1 : CY - 1, :]
        drop_inner[0:MID, lanes] = drop[1 + tile, 1 : CY - 1, :]
    fill_table(table_inner, INNER, sum_inner, code_inner, drop_inner)

    def pick_inner(base, size):
        for ref, found in zip(picked, pick(table_inner, INNER, INNER_AT, base, size)):
            ref[:, pl.ds(base, size)] = found

    for_blocks(pick_inner, block[2])

    from_left, from_right = SENT_BY[(1, 0)], SENT_BY[(-1, 0)]
    for copy in x_copies:
        copy.wait_recv()
    for flag, (own, code) in enumerate(((axis, code_outer), (drop, drop_outer))):
        code[0:MID, 0:NZ] = flag_x_got[from_left, flag, 1 : CY - 1, :]
        code[0:MID, NZ:COLS] = own[0, 1 : CY - 1, :]
        code[HALF : HALF + MID, 0:NZ] = own[CX - 1, 1 : CY - 1, :]
        code[HALF : HALF + MID, NZ:COLS] = flag_x_got[from_right, flag, 1 : CY - 1, :]
    both = [
        jnp.concatenate(
            [
                sum_outer[channel, 0:HALF, :] + outer_got[from_left, channel],
                sum_outer[channel, HALF:OUTER, :] + outer_got[from_right, channel],
            ],
            axis=0,
        )
        for channel in range(4)
    ]
    fill_table(table_outer, OUTER, both, code_outer, drop_outer)

    def pick_outer(base, size):
        for ref, found in zip(picked, pick(table_outer, OUTER, 0, base, size)):
            ref[:, pl.ds(base, size)] += found

    for_blocks(pick_outer, block[3])

    pl.when(first_in)(start_late)
    for copy in edge_copies + down_copies:
        copy.wait_recv()
    for pair in range(3):
        for side, end in enumerate((-1, 1)):
            ends = slice(side * 8, side * 8 + 8)
            whole = part_edge[pair, ends, :] + edge_y_got[SENT_BY[(0, -end)] - 2, pair]
            if pair != 1:
                step = 1 if pair == 0 else -1
                whole = whole + edge_x_got[SENT_BY[(step, 0)], ends, :]
                whole = whole + edge_d_got[SENT_BY[(step, -end)] - 4]
            for channel in range(4):
                at = pair * 4 + side * 2
                sum_edge[channel, at : at + 2, :] = whole[2 * channel : 2 * channel + 2]
            for tile in range(2):
                plane = 2 * pair + tile
                lanes = slice(tile * NZ, (tile + 1) * NZ)
                beyond = -1 if plane == 0 else 1 if plane == CX + 1 else 0
                last = CX - 1 if plane == 0 else 0 if plane == CX + 1 else plane - 1
                inside = 0 if side == 0 else CY - 1
                halo = flag_y_got.at[SENT_BY[(0, -end)] - 2]
                if beyond != 0:
                    halo = flag_d_got.at[SENT_BY[(-beyond, -end)] - 4]
                near = pair * 4 + (1 if side == 0 else 2)
                far = pair * 4 + (0 if side == 0 else 3)
                for flag, (own, code) in enumerate(((axis, code_edge), (drop, drop_edge))):
                    if beyond == 0:
                        value = own[last, inside : inside + 1, :]
                    else:
                        value = flag_x_got[SENT_BY[(-beyond, 0)], flag, inside : inside + 1, :]
                    code[near : near + 1, lanes] = value
                    code[far : far + 1, lanes] = halo[flag * CX + last : flag * CX + last + 1, :]
    fill_table(table_edge, EDGE, sum_edge, code_edge, drop_edge)

    cosine, sine = math.cos(ANGLE), math.sin(ANGLE)

    def finish(base, size):
        lanes = pl.ds(base, size)
        for ref, found in zip(picked, pick(table_edge, EDGE, EDGE_AT, base, size)):
            ref[:, lanes] += found
        mean = [picked[k][:, lanes] for k in range(3)]
        code = codes[:, lanes]
        rel = [vel[k][:, lanes] - mean[k] for k in range(3)]
        along_x = code < 1.5
        along_y = (code > 1.5) & (code < 3.5)
        along_z = code > 3.5
        odd = (code == 1.0) | (code == 3.0) | (code == 5.0)
        turn_by = jnp.where(odd, -sine, sine)
        plain = [cosine * r for r in rel]
        cross = [turn_by * r for r in rel]
        new_x = jnp.where(along_x, rel[0], plain[0] + jnp.where(along_y, cross[2], -cross[1]))
        new_y = jnp.where(along_y, rel[1], plain[1] + jnp.where(along_x, -cross[2], cross[0]))
        new_z = jnp.where(along_z, rel[2], plain[2] + jnp.where(along_x, cross[1], -cross[0]))
        living = rows[:, lanes] != NONE
        for k, new in enumerate((new_x, new_y, new_z)):
            outs[k][:, lanes] = jnp.where(living, mean[k] + new, 0.0)

    for_blocks(finish, block[4])

    stores = [
        pltpu.make_async_copy(outs[k], out_hbm.at[k : k + 1, :], load_sem.at[k]) for k in range(3)
    ]
    for store in stores:
        store.start()
    for copy in x_copies + edge_copies + down_copies:
        copy.wait_send()
    for store in stores:
        store.wait()


def body(positions, velocities, counts, grid_shift, axis_index, droplet):
    hbm = pl.BlockSpec(memory_space=pl.ANY)
    slots = positions.shape[1]
    block = BLOCK
    cells = (CX, CY, NZ)
    vmem = pltpu.VMEM
    return pl.pallas_call(
        functools.partial(kernel, block),
        out_shape=jax.ShapeDtypeStruct(velocities.shape, F32),
        in_specs=[hbm] * 6,
        out_specs=hbm,
        scratch_shapes=[
            pltpu.SMEM((1, 1), I32), pltpu.SMEM((3,), I32),
            *[vmem((1, slots), I32)] * 3, *[vmem((1, slots), F32)] * 3, vmem(cells, I32), vmem(cells, I32),
            *[vmem((1, slots), F32)] * 3,
            pltpu.SemaphoreType.DMA((10,)),
            vmem((1, slots), I32), vmem((COLS, slots), BF16), *[vmem((1, slots), F32)] * 4,
            vmem((7 * FIRST, COLS), F32), vmem((7 * INNER, COLS), F32),
            vmem((4, OUTER, COLS), F32), vmem((4, INNER, COLS), F32), vmem((4, EDGE, COLS), F32),
            vmem((3, 16, COLS), F32),
            vmem((7 * OUTER, COLS), BF16), vmem((7 * INNER, COLS), BF16), vmem((7 * EDGE, COLS), BF16),
            vmem((OUTER, COLS), I32), vmem((OUTER, COLS), I32),
            vmem((INNER, COLS), I32), vmem((INNER, COLS), I32),
            vmem((EDGE, COLS), I32), vmem((EDGE, COLS), I32),
            vmem((2, CY, NZ), I32), vmem((2, CY, NZ), I32),
            vmem((2 * CX, NZ), I32), vmem((2 * CX, NZ), I32),
            vmem((2, 2, CY, NZ), I32), vmem((2, 2 * CX, NZ), I32), vmem((4, 2 * CX, NZ), I32),
            vmem((2, 4, HALF, COLS), F32), vmem((2, 16, COLS), F32),
            vmem((2, 3, 8, COLS), F32), vmem((4, 8, COLS), F32),
            pltpu.SemaphoreType.DMA((18,)),
            pltpu.SemaphoreType.DMA((18,)),
            pltpu.SemaphoreType.REGULAR,
        ],
        compiler_params=pltpu.CompilerParams(
            collective_id=0, has_side_effects=True, vmem_limit_bytes=VMEM_MIB << 20
        ),
        name="collision_step",
    )(counts.reshape(1, 1), grid_shift, positions, velocities, axis_index, droplet)


BLOCK = (8192, 8192, 8192, 8192, 8192)
VMEM_MIB = 58


def solution(mesh):
    placed = (
        P(None, ("slab", "cross")),
        P(None, ("slab", "cross")),
        P(("slab", "cross")),
        P(),
        P("slab", "cross", None),
        P("slab", "cross", None),
    )
    return jax.shard_map(
        body, mesh=mesh, in_specs=placed, out_specs=P(None, ("slab", "cross")), check_vma=False
    )
```

time: 29.5 us -> 25.5 us (0.86)
  the two profiles are of different devices: /device:TPU:6 before, /device:TPU:448 now
where the time goes in v3:
time: 25.5 us; the launch traced here: 25.3 us
  Pallas kernels  22.9 us (90%)
  local copies, waits for them, and re-layouts  1.7 us (7%)
  between operations  0.66 us (3%)
    pallas_call x1, Pallas kernels, body(): pl.pallas_call(functools.partial(kernel, block), out_shape=jax.ShapeDtype...  22.9 us
    unnamed x1, local copies, waits for them, and re-layouts  1.7 us

profile of v3, /device:TPU:448, one launch (start us, length us, event | category | flops | bytes accessed | tf_op | source)
XLA Modules:
  0.0 25.3 jit_solution(12639972195759808797)
XLA Ops:
  0.7 22.9 %collision_step.1 = f32[3,16384]{1,0:T(4,128)} custom-call(s32[1,1]{1,0:T(1,128)} %bitcast.1.counts_in, s32[3]{0:T(128)} %shift_in.1, s32[3,16384]{1,0:T(4,128)} %pos_in.1, f32[3,16384]{1,0:T(4,128)} %vel_in.1, s32[4,32,128]{2,1,0:T(8,128)} %axis_in.1, s32[4,32,128]{2,1,0:T(8,128)} %drop_in.1), custom_call_target="tpu_custom_call" | custom-call | tf_op jit(solution)/shard_map/collision_step/pallas_call | solution.py:364
  23.6 1.7 %copy.9 = f32[3,16384]{1,0:T(4,128)} copy(f32[3,16384]{1,0:T(4,128)} %collision_step.1) | data formatting | bytes 393216

commit v4 on v3

--- a/solution.py
+++ b/solution.py
@@ -19,12 +19,11 @@
 
 CX, CY, NZ = 4, 32, 128
 COLS = 2 * NZ
-OUTER, EDGE, INNER = 64, 16, 32
-EDGE_AT = OUTER
-INNER_AT = OUTER + EDGE
-FIRST = OUTER + EDGE
+EDGE, SIDE = 16, 32
+HIGH_AT = EDGE
+LOW_AT = HIGH_AT + SIDE
+INNER_AT = LOW_AT + SIDE
 NONE = 127
-HALF = OUTER // 2
 MID = CY - 2
 
 STEPS = ((-1, 0), (1, 0), (0, -1), (0, 1), (-1, -1), (-1, 1), (1, -1), (1, 1))
@@ -46,12 +45,12 @@
     counts_in, shift_in, pos_in, vel_in, axis_in, drop_in, out_hbm,
     counts, shift, pos_x, pos_y, pos_z, vel_x, vel_y, vel_z, axis, drop, out_x, out_y, out_z, load_sem,
     rows, onehots, mean_x, mean_y, mean_z, codes,
-    acc_first, acc_inner, sum_outer, sum_inner, sum_edge, part_edge,
-    table_outer, table_inner, table_edge,
-    code_outer, drop_outer, code_inner, drop_inner, code_edge, drop_edge,
+    acc_first, acc_second, sum_low, sum_high, sum_inner, sum_edge, part_edge,
+    table_low, table_high, table_inner, table_edge,
+    code_low, drop_low, code_high, drop_high, code_inner, drop_inner, code_edge, drop_edge,
     flag_x_low, flag_x_high, flag_y_low, flag_y_high,
     flag_x_got, flag_y_got, flag_d_got,
-    outer_got, edge_x_got, edge_y_got, edge_d_got,
+    sums_got, edge_x_got, edge_y_got, edge_d_got,
     send_sem, recv_sem, late_sem,
 ):
     slots = rows.shape[1]
@@ -109,8 +108,10 @@
         lax.fori_loop(0, slots // size, run, 0)
 
     acc_first[...] = jnp.zeros_like(acc_first)
-    acc_inner[...] = jnp.zeros_like(acc_inner)
-    for ref in (code_outer, drop_outer, code_inner, drop_inner, code_edge, drop_edge, sum_edge):
+    acc_second[...] = jnp.zeros_like(acc_second)
+    for ref in (
+        code_low, drop_low, code_high, drop_high, code_inner, drop_inner, code_edge, drop_edge, sum_edge
+    ):
         ref[...] = jnp.zeros_like(ref)
 
     anchor_x = me_slab * (CX * QUANT)
@@ -129,8 +130,8 @@
         z = ((pos_z[:, lanes] + shift_z) >> 3) & (NZ - 1)
         pair = x >> 1
         at_low, at_high = y < 2, y >= CY
-        edge = pair * 4 + jnp.where(at_high, EDGE_AT - MID, EDGE_AT)
-        other = jnp.where(pair == 1, INNER_AT - 2, pair * (HALF // 2) - 2)
+        edge = pair * 4 + jnp.where(at_high, -MID, 0)
+        other = jnp.where(pair == 1, INNER_AT - 2, jnp.where(pair == 0, LOW_AT - 2, HIGH_AT - 2))
         row = jnp.where(at_low | at_high, edge, other) + y
         living = lax.broadcasted_iota(I32, (1, size), 1) + base < count
         row = jnp.where(living, row, NONE)
@@ -187,13 +188,10 @@
             found.append(jnp.sum(jnp.where(here, part, 0.0), axis=0, keepdims=True))
         return found
 
-    x_copies, edge_copies, down_copies = [], [], []
-    for index, step in enumerate(STEPS[:2]):
-        half = slice(0, HALF) if step[0] < 0 else slice(HALF, OUTER)
-        x_copies.append(remote(16 + index, sum_outer.at[:, half, :], outer_got.at[index], step))
-        source = flag_x_low if step[0] < 0 else flag_x_high
-        x_copies.append(remote(index, source, flag_x_got.at[index], step))
-    for index, step in sorted(enumerate(STEPS), key=lambda entry: -entry[1][1]):
+    to_below = remote(16, sum_low, sums_got.at[0], (-1, 0))
+    to_above = remote(17, sum_high, sums_got.at[1], (1, 0))
+    flag_copies, edge_copies, down_copies = [], [], []
+    for index, step in sorted(enumerate(STEPS), key=lambda entry: (-abs(entry[1][0] * entry[1][1]), -entry[1][1])):
         ends = slice(0, 16) if step[1] == 0 else slice(0, 8) if step[1] < 0 else slice(8, 16)
         if step[0] == 0:
             source, target = part_edge.at[:, ends, :], edge_y_got.at[index - 2]
@@ -202,9 +200,14 @@
             target = edge_x_got.at[index] if step[1] == 0 else edge_d_got.at[index - 4]
         into = down_copies if step[1] < 0 else edge_copies
         into.append(remote(8 + index, source, target, step))
-        if step[1] != 0:
+    for index, step in enumerate(STEPS):
+        if step[1] == 0:
+            source = flag_x_low if step[0] < 0 else flag_x_high
+            flag_copies.append(remote(index, source, flag_x_got.at[index], step))
+        else:
             source = flag_y_low if step[1] < 0 else flag_y_high
             target = flag_y_got.at[index - 2] if step[0] == 0 else flag_d_got.at[index - 4]
+            into = down_copies if step[1] < 0 else flag_copies
             into.append(remote(index, source, target, step))
 
     def start_down():
@@ -215,10 +218,11 @@
         pl.semaphore_wait(late_sem, 3)
         start_down()
 
-    for_blocks(functools.partial(deposit, acc_first, 0, FIRST), block[0])
+    first, second = EDGE + SIDE, 2 * SIDE
+    for_blocks(functools.partial(deposit, acc_first, 0, first), block[0])
     for channel in range(4):
-        sum_outer[channel] = total(acc_first, FIRST, channel, 0, OUTER)
-        edge = total(acc_first, FIRST, channel, EDGE_AT, EDGE)
+        sum_high[channel] = total(acc_first, first, channel, HIGH_AT, SIDE)
+        edge = total(acc_first, first, channel, 0, EDGE)
         for pair in range(3):
             for side in range(2):
                 at = side * 8 + channel * 2
@@ -239,54 +243,59 @@
     for copy in edge_copies:
         copy.start()
     pl.when(jnp.logical_not(first_in))(start_down)
-    for copy in x_copies:
+    for copy in flag_copies:
         copy.start()
+    to_above.start()
     pl.when(last_in)(lambda: greet(late_sem, (1,)))
 
-    for_blocks(functools.partial(deposit, acc_inner, INNER_AT, INNER), block[1])
+    for_blocks(functools.partial(deposit, acc_second, LOW_AT, second), block[1])
     for channel in range(4):
-        sum_inner[channel] = total(acc_inner, INNER, channel, 0, INNER)
+        sum_low[channel] = total(acc_second, second, channel, 0, SIDE)
+    to_below.start()
+    for channel in range(4):
+        sum_inner[channel] = total(acc_second, second, channel, SIDE, SIDE)
+
+    def pick_into(table, at, more, base, size):
+        for ref, found in zip(picked, pick(table, SIDE, at, base, size)):
+            lanes = pl.ds(base, size)
+            ref[:, lanes] = ref[:, lanes] + found if more else found
 
     for tile in range(2):
         lanes = slice(tile * NZ, (tile + 1) * NZ)
         code_inner[0:MID, lanes] = axis[1 + tile, 1 : CY - 1, :]
         drop_inner[0:MID, lanes] = drop[1 + tile, 1 : CY - 1, :]
-    fill_table(table_inner, INNER, sum_inner, code_inner, drop_inner)
-
-    def pick_inner(base, size):
-        for ref, found in zip(picked, pick(table_inner, INNER, INNER_AT, base, size)):
-            ref[:, pl.ds(base, size)] = found
-
-    for_blocks(pick_inner, block[2])
-
-    from_left, from_right = SENT_BY[(1, 0)], SENT_BY[(-1, 0)]
-    for copy in x_copies:
-        copy.wait_recv()
-    for flag, (own, code) in enumerate(((axis, code_outer), (drop, drop_outer))):
-        code[0:MID, 0:NZ] = flag_x_got[from_left, flag, 1 : CY - 1, :]
-        code[0:MID, NZ:COLS] = own[0, 1 : CY - 1, :]
-        code[HALF : HALF + MID, 0:NZ] = own[CX - 1, 1 : CY - 1, :]
-        code[HALF : HALF + MID, NZ:COLS] = flag_x_got[from_right, flag, 1 : CY - 1, :]
-    both = [
-        jnp.concatenate(
-            [
-                sum_outer[channel, 0:HALF, :] + outer_got[from_left, channel],
-                sum_outer[channel, HALF:OUTER, :] + outer_got[from_right, channel],
-            ],
-            axis=0,
-        )
-        for channel in range(4)
-    ]
-    fill_table(table_outer, OUTER, both, code_outer, drop_outer)
-
-    def pick_outer(base, size):
-        for ref, found in zip(picked, pick(table_outer, OUTER, 0, base, size)):
-            ref[:, pl.ds(base, size)] += found
-
-    for_blocks(pick_outer, block[3])
+    fill_table(table_inner, SIDE, sum_inner, code_inner, drop_inner)
+    for_blocks(functools.partial(pick_into, table_inner, INNER_AT, False), block[2])
+
+    from_below, from_above = SENT_BY[(1, 0)], SENT_BY[(-1, 0)]
+
+    def pick_low():
+        to_above.wait_recv()
+        flag_copies[from_below].wait_recv()
+        for flag, (own, code) in enumerate(((axis, code_low), (drop, drop_low))):
+            code[0:MID, 0:NZ] = flag_x_got[from_below, flag, 1 : CY - 1, :]
+            code[0:MID, NZ:COLS] = own[0, 1 : CY - 1, :]
+        both = [sum_low[channel] + sums_got[from_below, channel] for channel in range(4)]
+        fill_table(table_low, SIDE, both, code_low, drop_low)
+        for_blocks(functools.partial(pick_into, table_low, LOW_AT, True), block[3])
+
+    def pick_high():
+        to_below.wait_recv()
+        flag_copies[from_above].wait_recv()
+        for flag, (own, code) in enumerate(((axis, code_high), (drop, drop_high))):
+            code[0:MID, 0:NZ] = own[CX - 1, 1 : CY - 1, :]
+            code[0:MID, NZ:COLS] = flag_x_got[from_above, flag, 1 : CY - 1, :]
+        both = [sum_high[channel] + sums_got[from_above, channel] for channel in range(4)]
+        fill_table(table_high, SIDE, both, code_high, drop_high)
+        for_blocks(functools.partial(pick_into, table_high, HIGH_AT, True), block[3])
+
+    second_core = lax.rem(me_slab, 2) == 1
+    pl.when(jnp.logical_not(second_core))(pick_high)
+    pick_low()
+    pl.when(second_core)(pick_high)
 
     pl.when(first_in)(start_late)
-    for copy in edge_copies + down_copies:
+    for copy in edge_copies + flag_copies[2:] + down_copies:
         copy.wait_recv()
     for pair in range(3):
         for side, end in enumerate((-1, 1)):
@@ -323,7 +332,7 @@
 
     def finish(base, size):
         lanes = pl.ds(base, size)
-        for ref, found in zip(picked, pick(table_edge, EDGE, EDGE_AT, base, size)):
+        for ref, found in zip(picked, pick(table_edge, EDGE, 0, base, size)):
             ref[:, lanes] += found
         mean = [picked[k][:, lanes] for k in range(3)]
         code = codes[:, lanes]
@@ -349,7 +358,7 @@
     ]
     for store in stores:
         store.start()
-    for copy in x_copies + edge_copies + down_copies:
+    for copy in [to_below, to_above] + edge_copies + flag_copies + down_copies:
         copy.wait_send()
     for store in stores:
         store.wait()
@@ -372,17 +381,14 @@
             *[vmem((1, slots), F32)] * 3,
             pltpu.SemaphoreType.DMA((10,)),
             vmem((1, slots), I32), vmem((COLS, slots), BF16), *[vmem((1, slots), F32)] * 4,
-            vmem((7 * FIRST, COLS), F32), vmem((7 * INNER, COLS), F32),
-            vmem((4, OUTER, COLS), F32), vmem((4, INNER, COLS), F32), vmem((4, EDGE, COLS), F32),
-            vmem((3, 16, COLS), F32),
-            vmem((7 * OUTER, COLS), BF16), vmem((7 * INNER, COLS), BF16), vmem((7 * EDGE, COLS), BF16),
-            vmem((OUTER, COLS), I32), vmem((OUTER, COLS), I32),
-            vmem((INNER, COLS), I32), vmem((INNER, COLS), I32),
-            vmem((EDGE, COLS), I32), vmem((EDGE, COLS), I32),
+            vmem((7 * (EDGE + SIDE), COLS), F32), vmem((7 * 2 * SIDE, COLS), F32),
+            *[vmem((4, SIDE, COLS), F32)] * 3, vmem((4, EDGE, COLS), F32), vmem((3, 16, COLS), F32),
+            *[vmem((7 * SIDE, COLS), BF16)] * 3, vmem((7 * EDGE, COLS), BF16),
+            *[vmem((SIDE, COLS), I32)] * 6, *[vmem((EDGE, COLS), I32)] * 2,
             vmem((2, CY, NZ), I32), vmem((2, CY, NZ), I32),
             vmem((2 * CX, NZ), I32), vmem((2 * CX, NZ), I32),
             vmem((2, 2, CY, NZ), I32), vmem((2, 2 * CX, NZ), I32), vmem((4, 2 * CX, NZ), I32),
-            vmem((2, 4, HALF, COLS), F32), vmem((2, 16, COLS), F32),
+            vmem((2, 4, SIDE, COLS), F32), vmem((2, 16, COLS), F32),
             vmem((2, 3, 8, COLS), F32), vmem((4, 8, COLS), F32),
             pltpu.SemaphoreType.DMA((18,)),
             pltpu.SemaphoreType.DMA((18,)),
@@ -395,7 +401,7 @@
     )(counts.reshape(1, 1), grid_shift, positions, velocities, axis_index, droplet)
 
 
-BLOCK = (8192, 8192, 8192, 8192, 8192)
+BLOCK = (8192, 8192, 16384, 16384, 16384)
 VMEM_MIB = 58
 
 

time: 25.5 us -> 24.9 us (0.976)
  Pallas kernels: 22.9 us -> 22.4 us
    pallas_call x1, Pallas kernels: 22.9 us -> 22.4 us  [body(): pl.pallas_call(functools.partial(kernel, block), out_shape=jax.ShapeDtype...]
where the time goes in v4:
time: 24.9 us; the launch traced here: 24.7 us
  Pallas kernels  22.4 us (90%)
  local copies, waits for them, and re-layouts  1.7 us (7%)
  between operations  0.66 us (3%)
    pallas_call x1, Pallas kernels, body(): pl.pallas_call(functools.partial(kernel, block), out_shape=jax.ShapeDtype...  22.4 us
    unnamed x1, local copies, waits for them, and re-layouts  1.7 us

profile of v4, /device:TPU:448, one launch (start us, length us, event | category | flops | bytes accessed | tf_op | source)
XLA Modules:
  0.0 24.7 jit_solution(8730329569405001417)
XLA Ops:
  0.7 22.4 %collision_step.1 = f32[3,16384]{1,0:T(4,128)} custom-call(s32[1,1]{1,0:T(1,128)} %bitcast.1.counts_in, s32[3]{0:T(128)} %shift_in.1, s32[3,16384]{1,0:T(4,128)} %pos_in.1, f32[3,16384]{1,0:T(4,128)} %vel_in.1, s32[4,32,128]{2,1,0:T(8,128)} %axis_in.1, s32[4,32,128]{2,1,0:T(8,128)} %drop_in.1), custom_call_target="tpu_custom_call" | custom-call | tf_op jit(solution)/shard_map/collision_step/pallas_call | solution.py:373
  23.0 1.7 %copy.9 = f32[3,16384]{1,0:T(4,128)} copy(f32[3,16384]{1,0:T(4,128)} %collision_step.1) | data formatting | bytes 393216

commit v5 on v4

--- a/solution.py
+++ b/solution.py
@@ -51,7 +51,7 @@
     flag_x_low, flag_x_high, flag_y_low, flag_y_high,
     flag_x_got, flag_y_got, flag_d_got,
     sums_got, edge_x_got, edge_y_got, edge_d_got,
-    send_sem, recv_sem, late_sem,
+    send_sem, recv_sem, late_sem, row_sem,
 ):
     slots = rows.shape[1]
     vel = (vel_x, vel_y, vel_z)
@@ -81,13 +81,26 @@
     loads = [
         pltpu.make_async_copy(source, target, load_sem.at[index])
         for index, (source, target) in enumerate((
-            (counts_in, counts), (shift_in, shift),
-            (pos_in.at[0:1, :], pos_x), (pos_in.at[1:2, :], pos_y), (pos_in.at[2:3, :], pos_z),
-            (vel_in.at[0:1, :], vel_x), (vel_in.at[1:2, :], vel_y), (vel_in.at[2:3, :], vel_z),
-            (axis_in, axis), (drop_in, drop),
+            (counts_in, counts), (shift_in, shift), (axis_in, axis), (drop_in, drop),
         ))
     ]
-    for load in loads:
+
+    def load_rows(base, size):
+        lanes = pl.ds(base, size)
+        return [
+            pltpu.make_async_copy(
+                source.at[k : k + 1, lanes], target.at[:, lanes], row_sem.at[base // size, at + k]
+            )
+            for at, source, targets in ((0, pos_in, (pos_x, pos_y, pos_z)), (3, vel_in, vel))
+            for k, target in enumerate(targets)
+        ]
+
+    for load in loads[:2]:
+        load.start()
+    for base in range(0, slots, block[0]):
+        for load in load_rows(base, block[0]):
+            load.start()
+    for load in loads[2:]:
         load.start()
 
     def remote(index, source, target, step):
@@ -118,13 +131,15 @@
     anchor_y = me_cross * (CY * QUANT)
     period_x = slabs * CX * QUANT
     period_y = crosses * CY * QUANT
-    for load in loads[:8]:
+    for load in loads[:2]:
         load.wait()
     count = counts[0, 0]
     shift_x, shift_y, shift_z = shift[0], shift[1], shift[2]
 
     def find(base, size):
         lanes = pl.ds(base, size)
+        for load in load_rows(base, size):
+            load.wait()
         x = (((pos_x[:, lanes] - anchor_x + QUANT) & (period_x - 1)) + shift_x) >> 3
         y = (((pos_y[:, lanes] - anchor_y + QUANT) & (period_y - 1)) + shift_y) >> 3
         z = ((pos_z[:, lanes] + shift_z) >> 3) & (NZ - 1)
@@ -227,7 +242,7 @@
             for side in range(2):
                 at = side * 8 + channel * 2
                 part_edge[pair, at : at + 2, :] = edge[pair * 4 + side * 2 : pair * 4 + side * 2 + 2, :]
-    for load in loads[8:]:
+    for load in loads[2:]:
         load.wait()
     flag_x_low[0] = axis[0]
     flag_x_low[1] = drop[0]
@@ -393,6 +408,7 @@
             pltpu.SemaphoreType.DMA((18,)),
             pltpu.SemaphoreType.DMA((18,)),
             pltpu.SemaphoreType.REGULAR,
+            pltpu.SemaphoreType.DMA((slots // block[0], 6)),
         ],
         compiler_params=pltpu.CompilerParams(
             collective_id=0, has_side_effects=True, vmem_limit_bytes=VMEM_MIB << 20

time: 24.9 us -> 24.9 us (level)
  no operation moved by 1% of the time
where the time goes in v5:
time: 24.9 us; the launch traced here: 24.7 us
  Pallas kernels  22.3 us (90%)
  local copies, waits for them, and re-layouts  1.7 us (7%)
  between operations  0.66 us (3%)
    pallas_call x1, Pallas kernels, body(): pl.pallas_call(functools.partial(kernel, block), out_shape=jax.ShapeDtype...  22.3 us
    unnamed x1, local copies, waits for them, and re-layouts  1.7 us

profile of v5, /device:TPU:448, one launch (start us, length us, event | category | flops | bytes accessed | tf_op | source)
XLA Modules:
  0.0 24.7 jit_solution(11627946623950464652)
XLA Ops:
  0.7 22.3 %collision_step.1 = f32[3,16384]{1,0:T(4,128)} custom-call(s32[1,1]{1,0:T(1,128)} %bitcast.1.counts_in, s32[3]{0:T(128)} %shift_in.1, s32[3,16384]{1,0:T(4,128)} %pos_in.1, f32[3,16384]{1,0:T(4,128)} %vel_in.1, s32[4,32,128]{2,1,0:T(8,128)} %axis_in.1, s32[4,32,128]{2,1,0:T(8,128)} %drop_in.1), custom_call_target="tpu_custom_call" | custom-call | tf_op jit(solution)/shard_map/collision_step/pallas_call | solution.py:388
  23.0 1.7 %copy.9 = f32[3,16384]{1,0:T(4,128)} copy(f32[3,16384]{1,0:T(4,128)} %collision_step.1) | data formatting | bytes 393216
